TPU v7x, 32 devices: a whole 2x2x4 slice. The times are simulated.
32 devices in a mesh: gz: 2 (over x), xy: 16 (over z, y, core).
Axes of the slice: x: 2, y: 2, z: 4, core: 2. Of those that a mesh axis runs over, the one named last changes fastest.
Arguments:
- fixed: float32 [16, 256, 1024], P('gz', 'xy'), may hold values from -6 to 6
- moving: float32 [16, 256, 1024], P('gz', 'xy'), may hold values from -9 to 9
Outputs:
- update: float32 [3, 16, 256, 1024], P(None, 'gz', 'xy')
All inputs are finite; a program needn't handle non-finite values.
Results may differ from a plain program's by a relative error of at most 0.00016.
Values sent between devices are 32-bit elements; how exact they have to be, the bound alone decides.
A program may use at most 64 MiB of HBM per device.

v0:
```python
import jax
import jax.numpy as jnp
from jax import lax
from jax.sharding import PartitionSpec as P

RADIUS = 4
SPACING = 8


HIGH = lax.Precision.HIGHEST
EPS = 1e-05


def from_behind(block, axis, distance):
    devices = range(lax.axis_size(axis))
    route = [(i - distance, i) for i in devices if i - distance in devices]
    return lax.ppermute(block, axis, route)


def extended(block, sides, width):
    for axis, dim in sides:
        count = lax.axis_size(axis)
        forward = [(i, i + 1) for i in range(count - 1)]
        backward = [(target, source) for source, target in forward]
        low = lax.ppermute(
            lax.slice_in_dim(block, block.shape[dim] - width, None, axis=dim), axis, forward
        )
        high = lax.ppermute(lax.slice_in_dim(block, 0, width, axis=dim), axis, backward)
        block = jnp.concatenate([low, block, high], axis=dim)
    return block


def basis(index, knot):
    span = index // SPACING
    frac = (index - span * SPACING).astype(jnp.float32) / SPACING
    offset = knot - span
    other = 1.0 - frac
    first = other * other * other / 6.0
    second = (3.0 * frac**3 - 6.0 * frac**2 + 4.0) / 6.0
    third = (-3.0 * frac**3 + 3.0 * frac**2 + 3.0 * frac + 1.0) / 6.0
    fourth = frac**3 / 6.0
    zero = jnp.zeros_like(frac)
    return jnp.where(
        offset == 0,
        first,
        jnp.where(
            offset == 1, second, jnp.where(offset == 2, third, jnp.where(offset == 3, fourth, zero))
        ),
    )


def square_total(index):
    span = index // SPACING
    total = basis(index, span) ** 2
    for step in range(1, 4):
        total = total + basis(index, span + step) ** 2
    return total


def fit_matrix(index, knot):
    value = basis(index, knot)
    return value * value * value / square_total(index)


def knot_mass(knot, extent):
    spans = extent // SPACING
    within = jnp.arange(SPACING)
    offsets = jnp.arange(4)
    energy = jnp.sum(basis(within[None, :], offsets[:, None]) ** 2, axis=1)
    start = knot[:, None] - offsets[None, :]
    valid = (start >= 0) & (start <= spans - 1)
    return jnp.sum(jnp.where(valid, energy[None, :], jnp.zeros_like(energy)[None, :]), axis=1)


def window_sum(padded, shape):
    depth, rows, width = shape
    span = 2 * RADIUS + 1
    acc = padded[0:depth]
    for step in range(1, span):
        acc = acc + padded[step : step + depth]
    out = acc[:, 0:rows]
    for step in range(1, span):
        out = out + acc[:, step : step + rows]
    res = out[:, :, 0:width]
    for step in range(1, span):
        res = res + out[:, :, step : step + width]
    return res


def cc_force(fpad, mpad, shape):
    depth, rows, width = shape
    count = float((2 * RADIUS + 1) ** 3)
    sum_f = window_sum(fpad, shape)
    sum_m = window_sum(mpad, shape)
    sum_ff = window_sum(fpad * fpad, shape)
    sum_mm = window_sum(mpad * mpad, shape)
    sum_fm = window_sum(fpad * mpad, shape)
    r = RADIUS
    centre_f = fpad[r : r + depth, r : r + rows, r : r + width]
    centre_m = mpad[r : r + depth, r : r + rows, r : r + width]
    grad_z = (
        mpad[r + 1 : r + 1 + depth, r : r + rows, r : r + width]
        - mpad[r - 1 : r - 1 + depth, r : r + rows, r : r + width]
    ) * 0.5
    grad_y = (
        mpad[r : r + depth, r + 1 : r + 1 + rows, r : r + width]
        - mpad[r : r + depth, r - 1 : r - 1 + rows, r : r + width]
    ) * 0.5
    grad_x = (
        mpad[r : r + depth, r : r + rows, r + 1 : r + 1 + width]
        - mpad[r : r + depth, r : r + rows, r - 1 : r - 1 + width]
    ) * 0.5
    mean_f = sum_f / count
    mean_m = sum_m / count
    cov = sum_fm / count - mean_f * mean_m
    var_f = sum_ff / count - mean_f * mean_f
    var_m = sum_mm / count - mean_m * mean_m
    factor = 2.0 * cov / (var_f * var_m + EPS)
    resid = centre_f - mean_f - cov / (var_m + EPS) * (centre_m - mean_m)
    common = factor * resid
    return jnp.stack([common * grad_z, common * grad_y, common * grad_x])


def shifted_pads(block, offset):
    knots = block.shape[0]
    rest = ((0, 0),) * (block.ndim - 1)
    lower = ((0, offset),) + rest
    upper = ((offset, 0),) + rest
    return (lower, upper, knots)


def fold_rows(block, span, devices):
    reach = min((span + 2) // span, devices - 1)
    total = block
    for dist in range(1, reach + 1):
        offset = dist * span
        lower, upper, knots = shifted_pads(block, offset)
        below = from_behind(block, "xy", dist)
        above = from_behind(block, "xy", -dist)
        total = total + jnp.pad(below[offset:], lower) + jnp.pad(above[: knots - offset], upper)
    return total


def fold_planes(block, span, devices):
    reach = min((span + 2) // span, devices - 1)
    total = block
    for dist in range(1, reach + 1):
        offset = dist * span
        lower, upper, knots = shifted_pads(block, offset)
        below = from_behind(block, "gz", dist)
        above = from_behind(block, "gz", -dist)
        total = total + jnp.pad(below[offset:], lower) + jnp.pad(above[: knots - offset], upper)
    return total


def shards(fixed, moving):
    depth, rows, width = fixed.shape
    slab = lax.axis_index("gz")
    strip = lax.axis_index("xy")
    slabs_all = lax.axis_size("gz")
    strips_all = lax.axis_size("xy")
    span_z = depth // SPACING
    span_y = rows // SPACING
    knots_z = span_z + 3
    knots_y = span_y + 3
    knots_x = width // SPACING + 3
    stacked = jnp.stack([fixed, moving])
    rimmed = extended(stacked, (("gz", 1), ("xy", 2)), RADIUS)
    rimmed = jnp.pad(rimmed, ((0, 0), (0, 0), (0, 0), (RADIUS, RADIUS)))
    force = cc_force(rimmed[0], rimmed[1], (depth, rows, width))
    vox_x = jnp.arange(width)
    ctl_x = jnp.arange(knots_x)
    fit_x = fit_matrix(vox_x[:, None], ctl_x[None, :])
    reduced = jnp.dot(force.reshape(-1, width), fit_x, precision=HIGH).reshape(
        3, depth, rows, knots_x
    )
    vox_z = slab * depth + jnp.arange(depth)
    vox_y = strip * rows + jnp.arange(rows)
    ctl_z = slab * span_z + jnp.arange(knots_z)
    ctl_y = strip * span_y + jnp.arange(knots_y)
    own_fit_y = fit_matrix(vox_y[None, :], ctl_y[:, None])
    own_fit_z = fit_matrix(vox_z[None, :], ctl_z[:, None])
    plane_data = reduced.transpose(1, 0, 2, 3).reshape(depth, -1)
    plane_terms = jnp.dot(own_fit_z, plane_data, precision=HIGH).reshape(knots_z, 3, rows, knots_x)
    plane_block = fold_planes(plane_terms, span_z, slabs_all)
    row_data = plane_block.transpose(2, 0, 1, 3).reshape(rows, -1)
    row_terms = jnp.dot(own_fit_y, row_data, precision=HIGH).reshape(knots_y, knots_z, 3, knots_x)
    numer = fold_rows(row_terms, span_y, strips_all).transpose(1, 0, 2, 3)
    mass_z = knot_mass(ctl_z, depth * slabs_all)
    mass_y = knot_mass(ctl_y, rows * strips_all)
    mass_x = knot_mass(ctl_x, width)
    coef = numer / (
        mass_z[:, None, None, None] * mass_y[None, :, None, None] * mass_x[None, None, None, :]
    )
    eval_x = basis(vox_x[:, None], ctl_x[None, :])
    eval_y = basis(vox_y[:, None], ctl_y[None, :])
    eval_z = basis(vox_z[:, None], ctl_z[None, :])
    field = jnp.dot(coef.reshape(-1, knots_x), eval_x.T, precision=HIGH).reshape(
        knots_z, knots_y, 3, width
    )
    field = jnp.einsum("yb,abkx->aykx", eval_y, field, precision=HIGH)
    field = jnp.einsum("za,aykx->kzyx", eval_z, field, precision=HIGH)
    partial_power = jnp.sum(field * field)
    total_power = lax.psum(partial_power, ("gz", "xy"))
    power = total_power / (field.size * slabs_all * strips_all)
    return field / (jnp.sqrt(power) + 1e-06)


def solution(mesh):
    placed = (P("gz", "xy", None), P("gz", "xy", None))
    return jax.shard_map(
        shards, mesh=mesh, in_specs=placed, out_specs=P(None, "gz", "xy", None), check_vma=False
    )
```

profile of v0, /device:TPU:0, one launch (start us, length us, event | category | flops | bytes accessed | tf_op | source)
XLA Modules:
  0.0 128.6 jit_solution(14019872239903854002)
XLA Ops:
  0.0 1.3 %fusion.23 = (f32[2,4,16,1024]{3,2,1,0:T(8,128)S(1)}, f32[2,4,16,1024]{3,2,1,0:T(8,128)S(1)}) fusion(f32[1,8,16,1024]{3,2,1,0:T(8,128)} %bitcast.77, f32[1,8,16,1024]{3,2,1,0:T(8,128)} %bitcast.80), kind=kLoop, calls=%fused_computation.117 | loop fusion | flops 262144 | bytes 2097152 | tf_op jit(solution)/shard_map/stack | solution.py:167
  1.4 4.9 %collective-permute-start = (f32[2,4,16,1024]{3,2,1,0:T(8,128)S(1)}, f32[2,4,16,1024]{3,2,1,0:T(8,128)S(1)}, u32[]{:S(2)}, u32[]{:S(2)}) collective-permute-start(f32[2,4,16,1024]{3,2,1,0:T(8,128)S(1)} %get-tuple-element.18), channel_id=1, source_target_pairs={{0,16},{1,17},{2,18},{3,19},{4,20},{5,21},{6,22},{7,23},{8,24},{9,... | collective-permute-start | bytes 1572872 | tf_op jit(solution)/shard_map/ppermute | solution.py:25
  6.2 1.3 %collective-permute-start.1 = (f32[2,4,16,1024]{3,2,1,0:T(8,128)S(1)}, f32[2,4,16,1024]{3,2,1,0:T(8,128)S(1)}, u32[]{:S(2)}, u32[]{:S(2)}) collective-permute-start(f32[2,4,16,1024]{3,2,1,0:T(8,128)S(1)} %get-tuple-element.19), channel_id=1, source_target_pairs={{16,0},{17,1},{18,2},{19,3},{20,4},{21,5},{22,6},{23,7},{24,8},{25... | collective-permute-start | bytes 1572872 | tf_op jit(solution)/shard_map/ppermute | solution.py:28
  8.0 9.3 %collective-permute-done = f32[2,4,16,1024]{3,2,1,0:T(8,128)S(1)} collective-permute-done((f32[2,4,16,1024]{3,2,1,0:T(8,128)S(1)}, f32[2,4,16,1024]{3,2,1,0:T(8,128)S(1)}, u32[]{:S(2)}, u32[]{:S(2)}) %collective-permute-start) | collective-permute-done | bytes 524320 | tf_op jit(solution)/shard_map/ppermute | solution.py:25
  17.4 4.1 %collective-permute-done.1 = f32[2,4,16,1024]{3,2,1,0:T(8,128)S(1)} collective-permute-done((f32[2,4,16,1024]{3,2,1,0:T(8,128)S(1)}, f32[2,4,16,1024]{3,2,1,0:T(8,128)S(1)}, u32[]{:S(2)}, u32[]{:S(2)}) %collective-permute-start.1) | collective-permute-done | bytes 524320 | tf_op jit(solution)/shard_map/ppermute | solution.py:28
  21.8 1.3 %collective-permute-start.2 = (f32[2,16,4,1024]{3,2,1,0:T(4,128)S(1)}, f32[2,16,4,1024]{3,2,1,0:T(4,128)S(1)}, u32[]{:S(2)}, u32[]{:S(2)}) collective-permute-start(f32[2,16,4,1024]{3,2,1,0:T(4,128)S(1)} %get-tuple-element.16), channel_id=1, source_target_pairs={{0,1},{1,2},{2,3},{3,4},{4,5},{5,6},{6,7},{7,8},{8,9},{9,10},{10,1... | collective-permute-start | bytes 1572872 | tf_op jit(solution)/shard_map/ppermute | solution.py:25
  23.1 1.3 %collective-permute-start.3 = (f32[2,16,4,1024]{3,2,1,0:T(4,128)S(1)}, f32[2,16,4,1024]{3,2,1,0:T(4,128)S(1)}, u32[]{:S(2)}, u32[]{:S(2)}) collective-permute-start(f32[2,16,4,1024]{3,2,1,0:T(4,128)S(1)} %get-tuple-element.17), channel_id=1, source_target_pairs={{1,0},{2,1},{3,2},{4,3},{5,4},{6,5},{7,6},{8,7},{9,8},{10,9},{11,1... | collective-permute-start | bytes 1572872 | tf_op jit(solution)/shard_map/ppermute | solution.py:28
  24.8 3.9 %collective-permute-done.3 = f32[2,16,4,1024]{3,2,1,0:T(4,128)S(1)} collective-permute-done((f32[2,16,4,1024]{3,2,1,0:T(4,128)S(1)}, f32[2,16,4,1024]{3,2,1,0:T(4,128)S(1)}, u32[]{:S(2)}, u32[]{:S(2)}) %collective-permute-start.3) | collective-permute-done | bytes 524320 | tf_op jit(solution)/shard_map/ppermute | solution.py:28
  28.6 3.9 %select_maximum_fusion = f32[2,16,24,1032]{3,2,1,0:T(8,128)S(1)} fusion(f32[2,16,4,1024]{3,2,1,0:T(4,128)S(1)} %collective-permute-done.3, f32[2,16,4,1024]{3,2,1,0:T(4,128)S(1)} %collective-permute-done.2, f32[2,4,16,1024]{3,2,1,0:T(8,128)S(1)} %collective-permute-done.1, f32[2,4,16,1024]{3,2,1,0:T(8,128)S(1)} %collective-permute-done, ...), kind=kLoop, calls=%fused_computation.2 | loop fusion | flops 11096064 | bytes 6316032 | tf_op jit(solution)/shard_map/concatenate | solution.py:29
  32.9 0.5 fusion.11
  33.6 0.5 slice_add_fusion
  35.6 0.8 slice_add_fusion.56
  36.5 6.3 %fusion.32 = (f32[1,8,16,1024]{3,2,1,0:T(8,128)S(1)}, f32[8,16,1024]{2,1,0:T(8,128)S(1)}) fusion(f32[16,24,1032]{2,1,0:T(8,128)S(1)} %get-tuple-element.13, f32[16,24,1032]{2,1,0:T(8,128)S(1)} %get-tuple-element.12, f32[8,16,1032]{2,1,0:T(8,128)S(1)} %slice_add_fusion.40, f32[8,16,1032]{2,1,0:T(8,128)S(1)} %slice_add_fusion.48, ...), kind=kLoop, calls=%fused_computation.129 | loop fusion | flops 8519680 | bytes 26738688 | tf_op jit(solution)/shard_map/stack | solution.py:121
  42.8 0.6 fusion.29
  43.4 1.5 %fusion.7 = f32[8,3,16,131]{3,2,0,1:T(8,128)S(1)} fusion(f32[1,8,16,1024]{3,2,1,0:T(8,128)S(1)} %get-tuple-element.15, f32[1,8,16,1024]{3,2,1,0:T(8,128)S(1)} %get-tuple-element.14, f32[1,8,16,1024]{3,2,1,0:T(8,128)S(1)} %get-tuple-element.5, f32[1024]{0:T(1024)S(1)} %get-tuple-element.33, f32[1024]{0:T(1024)S(1)} %fusion.101, ...), kind=kOutput, calls=%fused_computation.19 | convolution fusion | flops 620531712 | bytes 1798656 | tf_op jit(solution)/shard_map/dot_general | solution.py:174
  45.2 0.4 dot_general.28
  45.6 0.7 fusion.47
  46.3 1.5 %collective-permute-start.4 = (f32[4,3,16,131]{3,0,2,1:T(4,128)S(1)}, f32[4,3,16,131]{3,0,2,1:T(4,128)S(1)}, u32[]{:S(2)}, u32[]{:S(2)}) collective-permute-start(f32[4,3,16,131]{3,0,2,1:T(4,128)S(1)} %fusion.47), channel_id=1, source_target_pairs={{0,16},{1,17},{2,18},{3,19},{4,20},{5,21},{6,22},{7,23},{8,24},{9,... | collective-permute-start | bytes 301832 | tf_op jit(solution)/shard_map/ppermute | solution.py:17
  47.8 1.3 %collective-permute-start.5 = (f32[4,3,16,131]{3,0,2,1:T(4,128)S(1)}, f32[4,3,16,131]{3,0,2,1:T(4,128)S(1)}, u32[]{:S(2)}, u32[]{:S(2)}) collective-permute-start(f32[4,3,16,131]{3,0,2,1:T(4,128)S(1)} %fusion.47), channel_id=1, source_target_pairs={{16,0},{17,1},{18,2},{19,3},{20,4},{21,5},{22,6},{23,7},{24,8},{25... | collective-permute-start | bytes 301832 | tf_op jit(solution)/shard_map/ppermute | solution.py:17
  49.1 1.8 %collective-permute-done.4 = f32[4,3,16,131]{3,0,2,1:T(4,128)S(1)} collective-permute-done((f32[4,3,16,131]{3,0,2,1:T(4,128)S(1)}, f32[4,3,16,131]{3,0,2,1:T(4,128)S(1)}, u32[]{:S(2)}, u32[]{:S(2)}) %collective-permute-start.4) | collective-permute-done | bytes 100640 | tf_op jit(solution)/shard_map/ppermute | solution.py:17
  51.0 4.3 %collective-permute-done.5 = f32[4,3,16,131]{3,0,2,1:T(4,128)S(1)} collective-permute-done((f32[4,3,16,131]{3,0,2,1:T(4,128)S(1)}, f32[4,3,16,131]{3,0,2,1:T(4,128)S(1)}, u32[]{:S(2)}, u32[]{:S(2)}) %collective-permute-start.5) | collective-permute-done | bytes 100640 | tf_op jit(solution)/shard_map/ppermute | solution.py:17
  56.5 9.0 %collective-permute-start.6 = (f32[5,4,3,131]{3,0,2,1:T(8,128)S(1)}, f32[5,4,3,131]{3,0,2,1:T(8,128)S(1)}, u32[]{:S(2)}, u32[]{:S(2)}) collective-permute-start(f32[5,4,3,131]{3,0,2,1:T(8,128)S(1)} %fusion.70), channel_id=1, source_target_pairs={{0,1},{1,2},{2,3},{3,4},{4,5},{5,6},{6,7},{7,8},{8,9},{9,10},{10,1... | collective-permute-start | bytes 94328 | tf_op jit(solution)/shard_map/ppermute | solution.py:17
  65.5 1.3 %collective-permute-start.7 = (f32[5,4,3,131]{3,0,2,1:T(8,128)S(1)}, f32[5,4,3,131]{3,0,2,1:T(8,128)S(1)}, u32[]{:S(2)}, u32[]{:S(2)}) collective-permute-start(f32[5,4,3,131]{3,0,2,1:T(8,128)S(1)} %fusion.70), channel_id=1, source_target_pairs={{1,0},{2,1},{3,2},{4,3},{5,4},{6,5},{7,6},{8,7},{9,8},{10,9},{11,1... | collective-permute-start | bytes 94328 | tf_op jit(solution)/shard_map/ppermute | solution.py:17
  66.8 7.9 %collective-permute-start.8 = (f32[5,4,3,131]{3,0,2,1:T(8,128)S(1)}, f32[5,4,3,131]{3,0,2,1:T(8,128)S(1)}, u32[]{:S(2)}, u32[]{:S(2)}) collective-permute-start(f32[5,4,3,131]{3,0,2,1:T(8,128)S(1)} %fusion.70), channel_id=1, source_target_pairs={{0,2},{1,3},{2,4},{3,5},{4,6},{5,7},{6,8},{7,9},{8,10},{9,11},{10,... | collective-permute-start | bytes 94328 | tf_op jit(solution)/shard_map/ppermute | solution.py:17
  74.8 1.3 %collective-permute-start.9 = (f32[5,4,3,131]{3,0,2,1:T(8,128)S(1)}, f32[5,4,3,131]{3,0,2,1:T(8,128)S(1)}, u32[]{:S(2)}, u32[]{:S(2)}) collective-permute-start(f32[5,4,3,131]{3,0,2,1:T(8,128)S(1)} %fusion.70), channel_id=1, source_target_pairs={{2,0},{3,1},{4,2},{5,3},{6,4},{7,5},{8,6},{9,7},{10,8},{11,9},{12,... | collective-permute-start | bytes 94328 | tf_op jit(solution)/shard_map/ppermute | solution.py:17
  76.2 0.8 collective-permute-done.8
  77.0 4.3 %collective-permute-done.9 = f32[5,4,3,131]{3,0,2,1:T(8,128)S(1)} collective-permute-done((f32[5,4,3,131]{3,0,2,1:T(8,128)S(1)}, f32[5,4,3,131]{3,0,2,1:T(8,128)S(1)}, u32[]{:S(2)}, u32[]{:S(2)}) %collective-permute-start.9) | collective-permute-done | bytes 31472 | tf_op jit(solution)/shard_map/ppermute | solution.py:17
  81.3 0.8 fusion.17
  82.1 0.9 convolution_bitcast_fusion
  83.0 2.9 %multiply_reduce_fusion = (f32[]{:T(128)}, f32[16,3,1024,8]{2,3,1,0:T(8,128)S(1)}) fusion(f32[8]{0:T(128)S(1)} %broadcast_multiply_fusion.3, f32[8]{0:T(128)S(1)} %get-tuple-element.24, f32[8]{0:T(128)S(1)} %get-tuple-element.25, f32[8]{0:T(128)S(1)} %get-tuple-element.22, s32[8]{0:T(128)S(1)} %and_select_fusion.1, s32[4]{0:T(128)S(1)} %iota_add_fusion.1, ...), kind=kOutput, calls=%fused_computation.17 | convolution fusion | flops 19661088 | bytes 2359476 | tf_op jit(solution)/shard_map/za,aykx->kzyx/dot_general | solution.py:202
  85.9 39.7 %psum.7 = f32[]{:T(128)} all-reduce(f32[]{:T(128)} %get-tuple-element.20), channel_id=1, replica_groups=mesh['gz'=2,'xy'=16] {'gz','xy'}, use_global_device_ids=true, to_apply=%region_5.6 | all-reduce | flops 1 | bytes 8 | tf_op jit(solution)/shard_map/psum | solution.py:204
  126.6 2.1 %copy.16 = f32[3,8,16,1024]{3,2,1,0:T(8,128)} copy(f32[3,8,16,1024]{3,1,0,2:T(8,128)S(1)} %divide_bitcast_fusion) | data formatting | bytes 3145728 | tf_op jit(solution)/shard_map/div | solution.py:206
  (50 shorter events, 4.9 us)
Async XLA Ops:
  0.0 21.5 %copy-start = (f32[8,16,1024]{2,1,0:T(8,128)S(1)}, f32[8,16,1024]{2,1,0:T(8,128)}, u32[]{:S(2)}) copy-start(f32[8,16,1024]{2,1,0:T(8,128)} %param.2) | copy-start | bytes 1572868
  0.0 21.5 %copy-start.1 = (f32[8,16,1024]{2,1,0:T(8,128)S(1)}, f32[8,16,1024]{2,1,0:T(8,128)}, u32[]{:S(2)}) copy-start(f32[8,16,1024]{2,1,0:T(8,128)} %param.3) | copy-start | bytes 1572868
  1.4 16.0 %collective-permute-start = (f32[2,4,16,1024]{3,2,1,0:T(8,128)S(1)}, f32[2,4,16,1024]{3,2,1,0:T(8,128)S(1)}, u32[]{:S(2)}, u32[]{:S(2)}) collective-permute-start(f32[2,4,16,1024]{3,2,1,0:T(8,128)S(1)} %get-tuple-element.18), channel_id=1, source_target_pairs={{0,16},{1,17},{2,18},{3,19},{4,20},{5,21},{6,22},{7,23},{8,24},{9,... | collective-permute-start | bytes 1572872 | tf_op jit(solution)/shard_map/ppermute | solution.py:25
  6.2 15.3 %collective-permute-start.1 = (f32[2,4,16,1024]{3,2,1,0:T(8,128)S(1)}, f32[2,4,16,1024]{3,2,1,0:T(8,128)S(1)}, u32[]{:S(2)}, u32[]{:S(2)}) collective-permute-start(f32[2,4,16,1024]{3,2,1,0:T(8,128)S(1)} %get-tuple-element.19), channel_id=1, source_target_pairs={{16,0},{17,1},{18,2},{19,3},{20,4},{21,5},{22,6},{23,7},{24,8},{25... | collective-permute-start | bytes 1572872 | tf_op jit(solution)/shard_map/ppermute | solution.py:28
  21.8 3.0 %collective-permute-start.2 = (f32[2,16,4,1024]{3,2,1,0:T(4,128)S(1)}, f32[2,16,4,1024]{3,2,1,0:T(4,128)S(1)}, u32[]{:S(2)}, u32[]{:S(2)}) collective-permute-start(f32[2,16,4,1024]{3,2,1,0:T(4,128)S(1)} %get-tuple-element.16), channel_id=1, source_target_pairs={{0,1},{1,2},{2,3},{3,4},{4,5},{5,6},{6,7},{7,8},{8,9},{9,10},{10,1... | collective-permute-start | bytes 1572872 | tf_op jit(solution)/shard_map/ppermute | solution.py:25
  23.1 5.5 %collective-permute-start.3 = (f32[2,16,4,1024]{3,2,1,0:T(4,128)S(1)}, f32[2,16,4,1024]{3,2,1,0:T(4,128)S(1)}, u32[]{:S(2)}, u32[]{:S(2)}) collective-permute-start(f32[2,16,4,1024]{3,2,1,0:T(4,128)S(1)} %get-tuple-element.17), channel_id=1, source_target_pairs={{1,0},{2,1},{3,2},{4,3},{5,4},{6,5},{7,6},{8,7},{9,8},{10,9},{11,1... | collective-permute-start | bytes 1572872 | tf_op jit(solution)/shard_map/ppermute | solution.py:28
  46.3 4.6 %collective-permute-start.4 = (f32[4,3,16,131]{3,0,2,1:T(4,128)S(1)}, f32[4,3,16,131]{3,0,2,1:T(4,128)S(1)}, u32[]{:S(2)}, u32[]{:S(2)}) collective-permute-start(f32[4,3,16,131]{3,0,2,1:T(4,128)S(1)} %fusion.47), channel_id=1, source_target_pairs={{0,16},{1,17},{2,18},{3,19},{4,20},{5,21},{6,22},{7,23},{8,24},{9,... | collective-permute-start | bytes 301832 | tf_op jit(solution)/shard_map/ppermute | solution.py:17
  47.8 7.6 %collective-permute-start.5 = (f32[4,3,16,131]{3,0,2,1:T(4,128)S(1)}, f32[4,3,16,131]{3,0,2,1:T(4,128)S(1)}, u32[]{:S(2)}, u32[]{:S(2)}) collective-permute-start(f32[4,3,16,131]{3,0,2,1:T(4,128)S(1)} %fusion.47), channel_id=1, source_target_pairs={{16,0},{17,1},{18,2},{19,3},{20,4},{21,5},{22,6},{23,7},{24,8},{25... | collective-permute-start | bytes 301832 | tf_op jit(solution)/shard_map/ppermute | solution.py:17
  56.5 19.7 %collective-permute-start.6 = (f32[5,4,3,131]{3,0,2,1:T(8,128)S(1)}, f32[5,4,3,131]{3,0,2,1:T(8,128)S(1)}, u32[]{:S(2)}, u32[]{:S(2)}) collective-permute-start(f32[5,4,3,131]{3,0,2,1:T(8,128)S(1)} %fusion.70), channel_id=1, source_target_pairs={{0,1},{1,2},{2,3},{3,4},{4,5},{5,6},{6,7},{7,8},{8,9},{9,10},{10,1... | collective-permute-start | bytes 94328 | tf_op jit(solution)/shard_map/ppermute | solution.py:17
  65.5 10.7 %collective-permute-start.7 = (f32[5,4,3,131]{3,0,2,1:T(8,128)S(1)}, f32[5,4,3,131]{3,0,2,1:T(8,128)S(1)}, u32[]{:S(2)}, u32[]{:S(2)}) collective-permute-start(f32[5,4,3,131]{3,0,2,1:T(8,128)S(1)} %fusion.70), channel_id=1, source_target_pairs={{1,0},{2,1},{3,2},{4,3},{5,4},{6,5},{7,6},{8,7},{9,8},{10,9},{11,1... | collective-permute-start | bytes 94328 | tf_op jit(solution)/shard_map/ppermute | solution.py:17
  66.8 10.1 %collective-permute-start.8 = (f32[5,4,3,131]{3,0,2,1:T(8,128)S(1)}, f32[5,4,3,131]{3,0,2,1:T(8,128)S(1)}, u32[]{:S(2)}, u32[]{:S(2)}) collective-permute-start(f32[5,4,3,131]{3,0,2,1:T(8,128)S(1)} %fusion.70), channel_id=1, source_target_pairs={{0,2},{1,3},{2,4},{3,5},{4,6},{5,7},{6,8},{7,9},{8,10},{9,11},{10,... | collective-permute-start | bytes 94328 | tf_op jit(solution)/shard_map/ppermute | solution.py:17
  74.8 6.5 %collective-permute-start.9 = (f32[5,4,3,131]{3,0,2,1:T(8,128)S(1)}, f32[5,4,3,131]{3,0,2,1:T(8,128)S(1)}, u32[]{:S(2)}, u32[]{:S(2)}) collective-permute-start(f32[5,4,3,131]{3,0,2,1:T(8,128)S(1)} %fusion.70), channel_id=1, source_target_pairs={{2,0},{3,1},{4,2},{5,3},{6,4},{7,5},{8,6},{9,7},{10,8},{11,9},{12,... | collective-permute-start | bytes 94328 | tf_op jit(solution)/shard_map/ppermute | solution.py:17
where the time goes:
time: 129 us
  blocking collectives  39.7 us (31%)
  starting transfers between devices  31.1 us (24%)
  waiting for transfers between devices  28.6 us (22%)
  other arithmetic  17.2 us (13%)
  matrix products  7.14 us (6%)
  local copies, waits for them, and re-layouts  3.78 us (3%)
    psum x1, blocking collectives, shards(): total_power = lax.psum(partial_power, ('gz', 'xy'))  39.7 us
    ppermute x6, starting transfers between devices, from_behind(): return lax.ppermute(block, axis, route)  22.3 us
    ppermute x6, waiting for transfers between devices, from_behind(): return lax.ppermute(block, axis, route)  11.3 us
    ppermute x2, waiting for transfers between devices, extended(): lax.ppermute(lax.slice_in_dim(block, block.shape[dim] - width, None, axis...  9.35 us
    ppermute x2, waiting for transfers between devices, extended(): lax.ppermute(lax.slice_in_dim(block, 0, width, axis=dim), axis, backward)  8.01 us
    another operation x2, other arithmetic, cc_force(): return jnp.stack([common * grad_z, common * grad_y, common * grad_x])  6.92 us
    ppermute x2, starting transfers between devices, extended(): lax.ppermute(lax.slice_in_dim(block, block.shape[dim] - width, None, axis...  6.2 us
    concatenate x1, other arithmetic, extended(): block = jnp.concatenate([low, block, high], axis=dim)  3.86 us
  transfers between devices with their start and end apart: 10, of which 7 were waited for; matrix products, arithmetic and copies ran while one was open for 1% of the time, Pallas kernels for 0%

commit v1 on v0

v1 whole, which is shorter than its diff:
```python
import functools

import jax
import jax.numpy as jnp
import numpy as np
from jax import lax
from jax.experimental import pallas as pl
from jax.experimental.pallas import tpu as pltpu
from jax.sharding import PartitionSpec as P

RADIUS = 4
SPACING = 8
HIGH = lax.Precision.HIGHEST
EPS = 1e-05
MESH = pl.DeviceIdType.MESH
LANE = 128


def np_basis(index, knot):
    span = index // SPACING
    t = (index - span * SPACING) / SPACING
    j = knot - span
    values = (
        (1 - t) ** 3 / 6,
        (3 * t**3 - 6 * t**2 + 4) / 6,
        (-3 * t**3 + 3 * t**2 + 3 * t + 1) / 6,
        t**3 / 6,
    )
    out = np.zeros(np.broadcast(index, knot).shape)
    for step in range(4):
        out = np.where(j == step, values[step], out)
    return out


def np_tables(extent):
    index = np.arange(extent)[:, None]
    value = np_basis(index, np.arange(extent // SPACING + 3)[None, :])
    return value, value**3 / (value**2).sum(axis=1, keepdims=True)


def energies():
    index = np.arange(SPACING)
    return [float((np_basis(index, np.full(SPACING, j)) ** 2).sum()) for j in range(4)]


def mass_of(knot, extent):
    total = jnp.zeros(knot.shape, jnp.float32)
    for j, energy in enumerate(energies()):
        start = knot - j
        total = total + jnp.where((start >= 0) & (start <= extent // SPACING - 1), energy, 0.0)
    return total


def group_size(count):
    size = 1
    while size * size < count and count % (size * 2) == 0:
        size *= 2
    return size


def dot(a, b):
    return jnp.dot(a, b, precision=HIGH, preferred_element_type=jnp.float32)


def kernel(
    n_z, n_y, depth, rows, width, group, ctl_pad,
    fitz_ref, f_hbm, m_hbm, fitx_hbm, evalx_hbm, gram_hbm, fity_ref, evalzy_ref,
    field_ref, scale_ref,
    img, packout, packin, ysum, grady, acc, fitx, evalx, gram, part, part_z, part_y,
    power_out, power_in,
    own_sem, const_sem, zs_sem, zr_sem, ys_sem, yr_sem, fs_sem, fr_sem,
    pzs_sem, pzr_sem, pys_sem, pyr_sem, ws_sem, wr_sem,
):
    r = RADIUS
    slab, strip = lax.axis_index("gz"), lax.axis_index("xy")
    span_z, span_y = depth // SPACING, rows // SPACING
    knots_z, knots_y = span_z + 3, span_y + 3
    reach_z = min((span_z + 2) // span_z, n_z - 1)
    reach_y = min((span_y + 2) // span_y, n_y - 1)
    pad_rows = fity_ref.shape[0] // knots_y
    up, down = slab < n_z - 1, slab > 0
    right, left = strip < n_y - 1, strip > 0
    after = rows + 2 * r

    own = [
        pltpu.make_async_copy(ref, img.at[i, pl.ds(r, depth)], own_sem.at[i])
        for i, ref in enumerate((f_hbm, m_hbm))
    ]
    consts = [
        pltpu.make_async_copy(src, dst, const_sem.at[i])
        for i, (src, dst) in enumerate(((fitx_hbm, fitx), (evalx_hbm, evalx), (gram_hbm, gram)))
    ]
    for copy in own:
        copy.start()

    barrier = pltpu.get_barrier_semaphore()
    lo_block = (strip // group) * group
    here = strip % group
    groups = n_y // group

    def beside(dist):
        if dist % group == 0:
            return []
        below = (strip >= dist) & (here < dist % group)
        above = (strip < n_y - dist) & (here >= group - dist % group)
        if dist > group:
            below, above = strip >= dist, strip < n_y - dist
        return [(below, strip - dist), (above, strip + dist)]

    def inner(step):
        place = (slab * group + here + step) % (n_z * group)
        return (place // group, lo_block + place % group)

    def outer(step):
        return (slab, (strip + step * group) % n_y)

    def greet(device):
        pl.semaphore_signal(barrier, inc=1, device_id=device, device_id_type=MESH)

    heard = n_z * group - 1 + groups - 1
    for step in range(1, n_z * group):
        greet(inner(step))
    for step in range(1, groups):
        greet(outer(step))
    for dist in range(1, reach_y + 1):
        for there, other in beside(dist):
            pl.when(there)(functools.partial(greet, (slab, other)))
            heard = heard + jnp.where(there, 1, 0)
    pl.semaphore_wait(barrier, heard)

    def zcopy(side, h, i):
        ref = (f_hbm, m_hbm)[i]
        src = h if side == 0 else depth - 1 - h
        dst = depth + r + h if side == 0 else r - 1 - h
        target = slab - 1 if side == 0 else slab + 1
        return pltpu.make_async_remote_copy(
            src_ref=ref.at[src], dst_ref=img.at[i, dst],
            send_sem=zs_sem.at[side, h, i], recv_sem=zr_sem.at[1 - side, h, i],
            device_id=(target, strip), device_id_type=MESH,
        )

    def zsends(act):
        for h in range(r):
            for i in range(2):
                pl.when(up)(lambda: act(zcopy(1, h, i)))
                pl.when(down)(lambda: act(zcopy(0, h, i)))

    zsends(lambda c: c.start())
    for copy in consts:
        copy.start()

    def zwait(side, h):
        plane = jnp.where(side == 0, r - 1 - h, depth + r + h)
        for i in range(2):
            pltpu.make_async_remote_copy(
                src_ref=img.at[i, plane], dst_ref=img.at[i, plane],
                send_sem=zs_sem.at[side, h, i], recv_sem=zr_sem.at[side, h, i],
                device_id=(slab, strip), device_id_type=MESH,
            ).wait_recv()

    def pack(plane):
        first = lax.broadcasted_iota(jnp.int32, (8, width), 0) < 4
        f0, m0 = img[0, plane, 0:8, :], img[1, plane, 0:8, :]
        f1, m1 = img[0, plane, rows - 8 : rows, :], img[1, plane, rows - 8 : rows, :]
        packout[0, plane] = jnp.where(first, m0, pltpu.roll(f0, 4, 0))
        packout[1, plane] = jnp.where(first, pltpu.roll(f1, 4, 0), m1)

    def ycopy(side):
        return pltpu.make_async_remote_copy(
            src_ref=packout.at[side, pl.ds(r, depth)], dst_ref=packin.at[1 - side, pl.ds(r, depth)],
            send_sem=ys_sem.at[side], recv_sem=yr_sem.at[1 - side],
            device_id=(slab, strip - 1 if side == 0 else strip + 1), device_id_type=MESH,
        )

    def fcopy(side, zside, h):
        plane = jnp.where(zside == 0, r - 1 - h, depth + r + h)
        return pltpu.make_async_remote_copy(
            src_ref=packout.at[side, plane], dst_ref=packin.at[1 - side, plane],
            send_sem=fs_sem.at[side, zside, h], recv_sem=fr_sem.at[1 - side, zside, h],
            device_id=(slab, strip - 1 if side == 0 else strip + 1), device_id_type=MESH,
        )

    def to_sides(act, make):
        pl.when(left)(lambda: act(make(0)))
        pl.when(right)(lambda: act(make(1)))

    def from_sides(make):
        pl.when(left)(lambda: make(1).wait_recv())
        pl.when(right)(lambda: make(0).wait_recv())

    for copy in own:
        copy.wait()

    def pack_own(p, carry):
        pack(p + r)
        return carry

    lax.fori_loop(0, depth, pack_own, 0)
    to_sides(lambda c: c.start(), ycopy)

    @pl.when(jnp.logical_not(left))
    def _():
        packin[0] = jnp.zeros_like(packin[0])

    @pl.when(jnp.logical_not(right))
    def _():
        packin[1] = jnp.zeros_like(packin[1])

    @pl.when(jnp.logical_not(down))
    def _():
        img[:, 0:r] = jnp.zeros((2, r, rows, width), jnp.float32)
        ysum[:, 0:r] = jnp.zeros((5, r, rows, width), jnp.float32)

    @pl.when(jnp.logical_not(up))
    def _():
        img[:, depth + r :] = jnp.zeros((2, r, rows, width), jnp.float32)
        ysum[:, depth + r :] = jnp.zeros((5, r, rows, width), jnp.float32)

    acc[...] = jnp.zeros_like(acc)

    chunk = 2 * LANE

    def rows_of(plane):
        first = lax.broadcasted_iota(jnp.int32, (8, chunk), 0) < 4
        filler = jnp.zeros((8, chunk), jnp.float32)
        for x in range(0, width, chunk):
            cols = slice(x, x + chunk)
            lo, hi = packin[0, plane, :, cols], packin[1, plane, :, cols]

            def around(i, low, high):
                t = pltpu.roll(jnp.concatenate([img[i, plane, :, cols], filler], axis=0), 4, 0)
                return jnp.concatenate(
                    [jnp.where(first, low, t[0:8]), t[8 : after - 8],
                     jnp.where(first, t[after - 8 :], high)], axis=0)

            f = around(0, lo, hi)
            m = around(1, pltpu.roll(lo, 4, 0), pltpu.roll(hi, 4, 0))
            for q, v in enumerate((f, m, f * f, m * m, f * m)):
                s = v + pltpu.roll(v, after - 1, 0)
                s = s + pltpu.roll(s, after - 2, 0)
                s = s + pltpu.roll(s, after - 4, 0)
                ysum[q, plane, :, cols] = s[0:rows] + v[8:after]
            diff = pltpu.roll(m, after - 5, 0) - pltpu.roll(m, after - 3, 0)
            grady[plane, :, cols] = diff[0:rows] * 0.5

    inv = 1.0 / float((2 * r + 1) ** 3)
    wide = width + LANE
    tail = jnp.zeros((8, LANE), jnp.float32)

    def force_of(z):
        for t in range(0, rows, 8):
            tile = slice(t, t + 8)
            sums = []
            for q in range(5):
                total = ysum[q, z, tile, :]
                for k in range(1, 2 * r + 1):
                    total = total + ysum[q, z + k, tile, :]
                total = jnp.concatenate([total, tail], axis=1)
                total = total + pltpu.roll(total, 1, 1) + pltpu.roll(total, wide - 1, 1)
                total = total + pltpu.roll(total, 3, 1) + pltpu.roll(total, wide - 3, 1)
                sums.append(total[:, 0:width] * inv)
            mean_f, mean_m, ff, mm, fm = sums
            cov = fm - mean_f * mean_m
            var_f = ff - mean_f * mean_f
            var_m = mm - mean_m * mean_m
            f, m = img[0, z + r, tile, :], img[1, z + r, tile, :]
            factor = 2.0 * cov / (var_f * var_m + EPS)
            resid = f - mean_f - cov / (var_m + EPS) * (m - mean_m)
            common = factor * resid
            mw = jnp.concatenate([m, tail], axis=1)
            gx = (pltpu.roll(mw, wide - 1, 1) - pltpu.roll(mw, 1, 1))[:, 0:width] * 0.5
            gz = (img[1, z + r + 1, tile, :] - img[1, z + r - 1, tile, :]) * 0.5
            gy = grady[z + r, tile, :]
            for k, g in enumerate((gz, gy, gx)):
                v = common * g
                for a in range(knots_z):
                    acc[a * 3 + k, tile, :] += v * fitz_ref[a, z]

    from_sides(ycopy)

    def own_rows(p, carry):
        rows_of(p + r)
        return carry

    lax.fori_loop(0, depth, own_rows, 0)

    @pl.when(jnp.logical_and(up, down))
    def _():
        def step(h, carry):
            zwait(0, h)
            pack(r - 1 - h)
            to_sides(lambda c: c.start(), lambda side: fcopy(side, 0, h))
            from_sides(lambda side: fcopy(side, 0, h))
            rows_of(r - 1 - h)
            return carry

        lax.fori_loop(0, r, step, 0)

    main = jnp.where(up, 1, 0)

    def place(s):
        return jnp.where(up, s, depth - 1 - s)

    def early(s, carry):
        force_of(place(s))
        return carry

    lax.fori_loop(0, depth - 2 * r, early, 0)

    def late(h, carry):
        plane = jnp.where(up, depth + r + h, r - 1 - h)
        zwait(main, h)
        pack(plane)
        to_sides(lambda c: c.start(), lambda side: fcopy(side, main, h))
        force_of(place(depth - 2 * r + h))
        from_sides(lambda side: fcopy(side, main, h))
        rows_of(plane)
        force_of(place(depth - r + h))
        return carry

    lax.fori_loop(0, r, late, 0)

    for copy in consts:
        copy.wait()
    reduced = dot(fity_ref[...], acc[...].reshape(knots_z * 3 * rows, width))
    block = dot(reduced, fitx[...])
    part[...] = block.reshape(part.shape)

    def pzcopy(side, dist):
        return pltpu.make_async_remote_copy(
            src_ref=part, dst_ref=part_z.at[1 - side, dist - 1],
            send_sem=pzs_sem.at[side, dist - 1], recv_sem=pzr_sem.at[1 - side, dist - 1],
            device_id=(slab - dist if side == 0 else slab + dist, strip), device_id_type=MESH,
        )

    def zfold(act_up, act_down):
        for dist in range(1, reach_z + 1):
            pl.when(slab < n_z - dist)(lambda: act_up(dist))
            pl.when(slab >= dist)(lambda: act_down(dist))

    zfold(lambda d: pzcopy(1, d).start(), lambda d: pzcopy(0, d).start())

    flat = (knots_y * pad_rows, ctl_pad)
    row_id = lax.broadcasted_iota(jnp.int32, flat, 0)
    inner_row = row_id % pad_rows
    knot_x = lax.broadcasted_iota(jnp.int32, flat, 1)
    used = (inner_row < knots_z * 3) & (knot_x < width // SPACING + 3)
    mass = (
        mass_of(slab * span_z + inner_row // 3, depth * n_z)
        * mass_of(strip * span_y + row_id // pad_rows, rows * n_y)
        * mass_of(knot_x, width)
    )
    weight = jnp.where(used, 1.0 / jnp.where(used, mass, 1.0), 0.0)

    zfold(lambda d: pzcopy(0, d).wait_recv(), lambda d: pzcopy(1, d).wait_recv())
    zfold(lambda d: pzcopy(1, d).wait_send(), lambda d: pzcopy(0, d).wait_send())
    for dist in range(1, reach_z + 1):
        offset = 3 * dist * span_z

        @pl.when(slab >= dist)
        def _():
            other = part_z[0, dist - 1].reshape(flat)
            moved = pltpu.roll(other, flat[0] - offset, 0)
            part[...] += jnp.where(inner_row < knots_z * 3 - offset, moved, 0.0).reshape(part.shape)

        @pl.when(slab < n_z - dist)
        def _():
            other = part_z[1, dist - 1].reshape(flat)
            moved = pltpu.roll(other, offset, 0)
            keep = (inner_row >= offset) & (inner_row < knots_z * 3)
            part[...] += jnp.where(keep, moved, 0.0).reshape(part.shape)

    def pycopy(side, dist):
        count = knots_y - dist * span_y
        start = 0 if side == 0 else dist * span_y
        return pltpu.make_async_remote_copy(
            src_ref=part.at[pl.ds(start, count)],
            dst_ref=part_y.at[1 - side, dist - 1, pl.ds(0, count)],
            send_sem=pys_sem.at[side, dist - 1], recv_sem=pyr_sem.at[1 - side, dist - 1],
            device_id=(slab, strip - dist if side == 0 else strip + dist), device_id_type=MESH,
        )

    def yfold(act_up, act_down):
        for dist in range(1, reach_y + 1):
            pl.when(strip < n_y - dist)(lambda: act_up(dist))
            pl.when(strip >= dist)(lambda: act_down(dist))

    yfold(lambda d: pycopy(1, d).start(), lambda d: pycopy(0, d).start())
    yfold(lambda d: pycopy(0, d).wait_recv(), lambda d: pycopy(1, d).wait_recv())
    yfold(lambda d: pycopy(1, d).wait_send(), lambda d: pycopy(0, d).wait_send())
    for dist in range(1, reach_y + 1):
        count = knots_y - dist * span_y

        @pl.when(strip >= dist)
        def _():
            part[0:count] += part_y[0, dist - 1, 0:count]

        @pl.when(strip < n_y - dist)
        def _():
            part[knots_y - count :] += part_y[1, dist - 1, 0:count]

    coef = part[...].reshape(flat) * weight
    lines = dot(evalzy_ref[...], coef)
    power = jnp.sum(lines * dot(lines, gram[...]))
    power_out[0] = jnp.full((8, LANE), power, jnp.float32)

    size = n_z * group

    def wcopy(step, stage):
        slot = step - 1 if stage == 0 else size - 1 + step - 1
        return pltpu.make_async_remote_copy(
            src_ref=power_out.at[stage], dst_ref=power_in.at[slot],
            send_sem=ws_sem.at[slot], recv_sem=wr_sem.at[slot],
            device_id=inner(step) if stage == 0 else outer(step), device_id_type=MESH,
        )

    for step in range(1, size):
        wcopy(step, 0).start()
    lines_per = lines.shape[0] // 3
    for k in range(3):
        field_ref[k] = dot(lines[k * lines_per : (k + 1) * lines_per], evalx[...]).reshape(
            depth, rows, width)
    total = power_out[0]
    for step in range(1, size):
        wcopy(step, 0).wait_recv()
    for step in range(1, size):
        total = total + power_in[step - 1]
    power_out[1] = total
    for step in range(1, groups):
        wcopy(step, 1).start()
    for step in range(1, size):
        wcopy(step, 0).wait_send()
    zsends(lambda c: c.wait_send())
    to_sides(lambda c: c.wait_send(), ycopy)

    def sent(zside):
        def step(h, carry):
            to_sides(lambda c: c.wait_send(), lambda side: fcopy(side, zside, h))
            return carry

        lax.fori_loop(0, r, step, 0)

    pl.when(up)(lambda: sent(1))
    pl.when(down)(lambda: sent(0))

    for step in range(1, groups):
        wcopy(step, 1).wait_recv()
    for step in range(1, groups):
        total = total + power_in[size - 1 + step - 1]
    for step in range(1, groups):
        wcopy(step, 1).wait_send()
    entries = float(3 * depth * rows * width) * n_z * n_y
    scale_ref[...] = 1.0 / (jnp.sqrt(total / entries) + 1e-06)


def shards(n_z, n_y, fixed, moving):
    depth, rows, width = fixed.shape
    r = RADIUS
    eval_z, fit_z = np_tables(depth)
    eval_y, fit_y = np_tables(rows)
    eval_x, fit_x = np_tables(width)
    knots_z, knots_y, knots_x = eval_z.shape[1], eval_y.shape[1], eval_x.shape[1]
    lines = knots_z * 3
    pad_rows = -(-lines // 8) * 8
    ctl_pad = -(-knots_x // LANE) * LANE
    f32 = np.float32
    fitx = np.zeros((width, ctl_pad))
    fitx[:, :knots_x] = fit_x
    evalx = np.zeros((ctl_pad, width))
    evalx[:knots_x] = eval_x.T
    gram = evalx @ evalx.T
    fity = np.zeros((knots_y, pad_rows, lines, rows))
    for line in range(lines):
        fity[:, line, line, :] = fit_y.T
    fity = fity.reshape(knots_y * pad_rows, lines * rows)
    evalzy = np.zeros((3, depth, rows, knots_y, pad_rows))
    for k in range(3):
        for a in range(knots_z):
            evalzy[k, :, :, :, a * 3 + k] = eval_z[:, a][:, None, None] * eval_y[None]
    evalzy = evalzy.reshape(3 * depth * rows, knots_y * pad_rows)
    group = group_size(n_y)
    slots = n_z * group - 1 + n_y // group - 1
    reach_z = min((depth // SPACING + 2) // (depth // SPACING), n_z - 1)
    reach_y = min((rows // SPACING + 2) // (rows // SPACING), n_y - 1)
    dma = pltpu.SemaphoreType.DMA
    vmem = functools.partial(pltpu.VMEM, dtype=jnp.float32)
    block = (knots_y, pad_rows, ctl_pad)
    anywhere = pl.BlockSpec(memory_space=pl.ANY)
    inside = pl.BlockSpec(memory_space=pltpu.VMEM)
    field, scale = pl.pallas_call(
        functools.partial(kernel, n_z, n_y, depth, rows, width, group, ctl_pad),
        out_shape=(
            jax.ShapeDtypeStruct((3, depth, rows, width), jnp.float32),
            jax.ShapeDtypeStruct((8, LANE), jnp.float32),
        ),
        in_specs=[pl.BlockSpec(memory_space=pltpu.SMEM)] + [anywhere] * 5 + [inside] * 2,
        out_specs=(inside, inside),
        scratch_shapes=[
            vmem((2, depth + 2 * r, rows, width)),
            vmem((2, depth + 2 * r, 8, width)),
            vmem((2, depth + 2 * r, 8, width)),
            vmem((5, depth + 2 * r, rows, width)),
            vmem((depth + 2 * r, rows, width)),
            vmem((lines, rows, width)),
            vmem((width, ctl_pad)),
            vmem((ctl_pad, width)),
            vmem((ctl_pad, ctl_pad)),
            vmem(block),
            vmem((2, reach_z) + block),
            vmem((2, reach_y) + block),
            vmem((2, 8, LANE)),
            vmem((slots, 8, LANE)),
            dma((2,)), dma((3,)),
            dma((2, r, 2)), dma((2, r, 2)),
            dma((2,)), dma((2,)),
            dma((2, 2, r)), dma((2, 2, r)),
            dma((2, reach_z)), dma((2, reach_z)),
            dma((2, reach_y)), dma((2, reach_y)),
            dma((slots,)), dma((slots,)),
        ],
        compiler_params=pltpu.CompilerParams(
            collective_id=0, has_side_effects=True, vmem_limit_bytes=48 * 1024 * 1024
        ),
        cost_estimate=pl.CostEstimate(flops=10**9, bytes_accessed=10**7, transcendentals=0),
    )(
        jnp.asarray(fit_z.T.astype(f32)), fixed, moving, jnp.asarray(fitx.astype(f32)),
        jnp.asarray(evalx.astype(f32)), jnp.asarray(gram.astype(f32)),
        jnp.asarray(fity.astype(f32)), jnp.asarray(evalzy.astype(f32)),
    )
    return field * scale[0, 0]


def solution(mesh):
    placed = (P("gz", "xy", None), P("gz", "xy", None))
    return jax.shard_map(
        functools.partial(shards, mesh.shape["gz"], mesh.shape["xy"]), mesh=mesh, in_specs=placed,
        out_specs=P(None, "gz", "xy", None), check_vma=False
    )
```

time: 129 us -> 57.9 us (0.45)
  Pallas kernels: 0 us -> 47 us
  blocking collectives: 39.7 us -> 0 us
  starting transfers between devices: 31.1 us -> 0 us
  waiting for transfers between devices: 28.6 us -> 0 us
  other arithmetic: 17.2 us -> 1.93 us
  matrix products: 7.14 us -> 0 us
  local copies, waits for them, and re-layouts: 3.78 us -> 8.55 us
    pallas_call x0 -> x1, Pallas kernels: none -> 47 us  [shards(): pl.pallas_call(functools.partial(kernel, n_z, n_y, depth, rows, width, gr...]
    psum x1 -> x0, blocking collectives: 39.7 us -> none  [shards(): total_power = lax.psum(partial_power, ('gz', 'xy'))]
    ppermute x10 -> x0, starting transfers between devices: 31.1 us -> none  [the longest x6 22.3 us: from_behind(): return lax.ppermute(block, axis, route)]
    ppermute x10 -> x0, waiting for transfers between devices: 28.6 us -> none  [the longest x6 11.3 us: from_behind(): return lax.ppermute(block, axis, route)]
    another operation x3 -> x0, other arithmetic: 8.27 us -> none  [the longest x2 6.92 us: cc_force(): return jnp.stack([common * grad_z, common * grad_y, common * grad_x])]
    unnamed x4 -> x16, local copies, waits for them, and re-layouts: 0.01 us -> 7.97 us
    dot_general x6 -> x0, matrix products: 7.14 us -> none  [the longest x1 2.9 us: shards(): field = jnp.einsum('za,aykx->kzyx', eval_z, field, precision=HIGH)]
    concatenate x1 -> x0, other arithmetic: 3.86 us -> none  [extended(): block = jnp.concatenate([low, block, high], axis=dim)]
  transfers between devices with their start and end apart: 10 -> 0, of which waited for: 7 -> 0; matrix products, arithmetic and copies ran while one was open for 1% -> 0% of each run, Pallas kernels for 0% -> 0%
where the time goes in v1:
time: 57.9 us; the launch traced here: 57.5 us
  Pallas kernels  47 us (81%)
  local copies, waits for them, and re-layouts  8.55 us (15%)
  other arithmetic  1.93 us (3%)
    pallas_call x1, Pallas kernels, shards(): pl.pallas_call(functools.partial(kernel, n_z, n_y, depth, rows, width, gr...  47 us
    unnamed x16, local copies, waits for them, and re-layouts  7.97 us
    mul x1, other arithmetic, shards(): return field * scale[0, 0]  1.93 us

profile of v1, /device:TPU:0, one launch (start us, length us, event | category | flops | bytes accessed | tf_op | source)
XLA Modules:
  0.0 57.5 jit_solution(11613282682941873988)
XLA Ops:
  0.0 0.0 copy-start
  0.0 1.0 %copy-done = f32[8,16,1024]{2,1,0:T(8,128)S(1)} copy-done((f32[8,16,1024]{2,1,0:T(8,128)S(1)}, f32[8,16,1024]{2,1,0:T(8,128)}, u32[]{:S(2)}) %copy-start) | copy-done | bytes 524312
  1.0 0.0 copy-start.1
  1.0 1.0 %copy-done.1 = f32[8,16,1024]{2,1,0:T(8,128)S(1)} copy-done((f32[8,16,1024]{2,1,0:T(8,128)S(1)}, f32[8,16,1024]{2,1,0:T(8,128)}, u32[]{:S(2)}) %copy-start.1) | copy-done | bytes 524312
  2.1 0.0 copy-start.2
  2.1 1.2 %copy-done.2 = f32[256,1024]{1,0:T(8,128)S(1)} copy-done((f32[256,1024]{1,0:T(8,128)S(1)}, f32[256,1024]{1,0:T(8,128)}, u32[]{:S(2)}) %copy-start.2) | copy-done | bytes 1048600
  3.3 0.0 copy-start.3
  3.3 1.2 %copy-done.3 = f32[1024,256]{1,0:T(8,128)S(1)} copy-done((f32[1024,256]{1,0:T(8,128)S(1)}, f32[1024,256]{1,0:T(8,128)}, u32[]{:S(2)}) %copy-start.3) | copy-done | bytes 1048600
  4.5 0.0 copy-start.4
  4.5 0.9 %copy-done.4 = f32[256,256]{1,0:T(8,128)S(1)} copy-done((f32[256,256]{1,0:T(8,128)S(1)}, f32[256,256]{1,0:T(8,128)}, u32[]{:S(2)}) %copy-start.4) | copy-done | bytes 262168
  5.5 0.0 copy-start.5
  5.5 0.9 %copy-done.5 = f32[384,80]{1,0:T(8,128)S(1)} copy-done((f32[384,80]{1,0:T(8,128)S(1)}, f32[384,80]{1,0:T(8,128)}, u32[]{:S(2)}) %copy-start.5) | copy-done | bytes 122904
  6.4 0.0 copy-start.6
  6.4 0.9 %copy-done.6 = f32[80,192]{1,0:T(8,128)S(1)} copy-done((f32[80,192]{1,0:T(8,128)S(1)}, f32[80,192]{1,0:T(8,128)}, u32[]{:S(2)}) %copy-start.6) | copy-done | bytes 61464
  7.3 0.0 copy-start.7
  7.3 0.7 %copy-done.7 = f32[4,8]{1,0:T(4,128)S(1)} copy-done((f32[4,8]{1,0:T(4,128)S(1)}, f32[4,8]{1,0:T(4,128)}, u32[]{:S(2)}) %copy-start.7) | copy-done | bytes 152
  8.0 47.0 %shard_map.82 = (f32[3,8,16,1024]{3,2,1,0:T(8,128)S(1)}, f32[8,128]{1,0:T(8,128)S(1)}) custom-call(f32[4,8]{1,0:T(4,128)S(1)} %copy-done.7, f32[8,16,1024]{2,1,0:T(8,128)S(1)} %copy-done, f32[8,16,1024]{2,1,0:T(8,128)S(1)} %copy-done.1, f32[1024,256]{1,0:T(8,128)S(1)} %copy-done.3, f32[256,1024]{1,0:T(8,128)S(1)} %copy-done.2, f32[256,256]{1,0:T(8,128)S(1)} %copy-done.4, ...), custom_call_target="tpu_custom_call" | custom-call | flops 1000000000 | bytes 10000000 | tf_op jit(solution)/shard_map/pallas_call | solution.py:490
  55.0 0.6 %slice.3 = f32[1,1]{1,0:T(1,128)} slice(f32[8,128]{1,0:T(8,128)S(1)} %get-tuple-element.8), slice={[0:1], [0:1]} | slice | bytes 8 | tf_op jit(solution)/shard_map/slice | solution.py:530
  55.6 1.9 %broadcast_multiply_fusion = f32[3,8,16,1024]{3,2,1,0:T(8,128)} fusion(f32[3,8,16,1024]{3,2,1,0:T(8,128)S(1)} %get-tuple-element.7, f32[]{:T(128)} %bitcast), kind=kLoop, calls=%fused_computation | loop fusion | flops 393216 | bytes 3145732 | tf_op jit(solution)/shard_map/mul | solution.py:530
Async XLA Ops:
  0.0 1.0 %copy-start = (f32[8,16,1024]{2,1,0:T(8,128)S(1)}, f32[8,16,1024]{2,1,0:T(8,128)}, u32[]{:S(2)}) copy-start(f32[8,16,1024]{2,1,0:T(8,128)} %f_hbm.1) | copy-start | bytes 1572868
  1.0 1.0 %copy-start.1 = (f32[8,16,1024]{2,1,0:T(8,128)S(1)}, f32[8,16,1024]{2,1,0:T(8,128)}, u32[]{:S(2)}) copy-start(f32[8,16,1024]{2,1,0:T(8,128)} %m_hbm.1) | copy-start | bytes 1572868
  2.1 1.2 %copy-start.2 = (f32[256,1024]{1,0:T(8,128)S(1)}, f32[256,1024]{1,0:T(8,128)}, u32[]{:S(2)}) copy-start(f32[256,1024]{1,0:T(8,128)} %constant.14.clone.evalx_hbm) | copy-start | bytes 3145732
  3.3 1.2 %copy-start.3 = (f32[1024,256]{1,0:T(8,128)S(1)}, f32[1024,256]{1,0:T(8,128)}, u32[]{:S(2)}) copy-start(f32[1024,256]{1,0:T(8,128)} %constant.13.clone.fitx_hbm) | copy-start | bytes 3145732
  4.5 0.9 %copy-start.4 = (f32[256,256]{1,0:T(8,128)S(1)}, f32[256,256]{1,0:T(8,128)}, u32[]{:S(2)}) copy-start(f32[256,256]{1,0:T(8,128)} %constant.15.clone.gram_hbm) | copy-start | bytes 786436
  5.5 0.9 %copy-start.5 = (f32[384,80]{1,0:T(8,128)S(1)}, f32[384,80]{1,0:T(8,128)}, u32[]{:S(2)}) copy-start(f32[384,80]{1,0:T(8,128)} %constant.17.clone.evalzy_ref) | copy-start | bytes 368644
  6.4 0.9 %copy-start.6 = (f32[80,192]{1,0:T(8,128)S(1)}, f32[80,192]{1,0:T(8,128)}, u32[]{:S(2)}) copy-start(f32[80,192]{1,0:T(8,128)} %constant.16.clone.fity_ref) | copy-start | bytes 184324
  7.3 0.7 %copy-start.7 = (f32[4,8]{1,0:T(4,128)S(1)}, f32[4,8]{1,0:T(4,128)}, u32[]{:S(2)}) copy-start(f32[4,8]{1,0:T(4,128)} %constant.12.clone.fitz_ref) | copy-start | bytes 388

commit v2 on v1

--- a/solution.py
+++ b/solution.py
@@ -10,7 +10,6 @@
 
 RADIUS = 4
 SPACING = 8
-HIGH = lax.Precision.HIGHEST
 EPS = 1e-05
 MESH = pl.DeviceIdType.MESH
 LANE = 128
@@ -59,14 +58,29 @@
 
 
 def dot(a, b):
-    return jnp.dot(a, b, precision=HIGH, preferred_element_type=jnp.float32)
+    return jnp.dot(a, b, preferred_element_type=jnp.float32)
+
+
+def halves(x):
+    high = x.astype(jnp.bfloat16)
+    return high, (x - high.astype(jnp.float32)).astype(jnp.bfloat16)
+
+
+def np_halves(x):
+    x = x.astype(np.float32)
+    high = x.astype(jnp.bfloat16)
+    return high, (x - high.astype(np.float32)).astype(jnp.bfloat16)
+
+
+def dot3(a, b):
+    return dot(a[0], b[0]) + (dot(a[1], b[0]) + dot(a[0], b[1]))
 
 
 def kernel(
     n_z, n_y, depth, rows, width, group, ctl_pad,
-    fitz_ref, f_hbm, m_hbm, fitx_hbm, evalx_hbm, gram_hbm, fity_ref, evalzy_ref,
+    f_hbm, m_hbm, fitx_hbm, evalx_hbm, fity_hbm, evalzy_hbm, gram_hbm,
     field_ref, scale_ref,
-    img, packout, packin, ysum, grady, acc, fitx, evalx, gram, part, part_z, part_y,
+    img, packout, packin, ysum, grady, acc, fitx, evalx, fity, evalzy, gram, fitz, part, part_z, part_y,
     power_out, power_in,
     own_sem, const_sem, zs_sem, zr_sem, ys_sem, yr_sem, fs_sem, fr_sem,
     pzs_sem, pzr_sem, pys_sem, pyr_sem, ws_sem, wr_sem,
@@ -77,7 +91,7 @@
     knots_z, knots_y = span_z + 3, span_y + 3
     reach_z = min((span_z + 2) // span_z, n_z - 1)
     reach_y = min((span_y + 2) // span_y, n_y - 1)
-    pad_rows = fity_ref.shape[0] // knots_y
+    pad_rows = fity.shape[1] // knots_y
     up, down = slab < n_z - 1, slab > 0
     right, left = strip < n_y - 1, strip > 0
     after = rows + 2 * r
@@ -88,10 +102,19 @@
     ]
     consts = [
         pltpu.make_async_copy(src, dst, const_sem.at[i])
-        for i, (src, dst) in enumerate(((fitx_hbm, fitx), (evalx_hbm, evalx), (gram_hbm, gram)))
+        for i, (src, dst) in enumerate(
+            ((fitx_hbm, fitx), (evalx_hbm, evalx), (fity_hbm, fity), (evalzy_hbm, evalzy),
+             (gram_hbm, gram))
+        )
     ]
     for copy in own:
         copy.start()
+    for copy in consts:
+        copy.start()
+    fit_table = np_tables(depth)[1]
+    for a in range(knots_z):
+        for z in range(depth):
+            fitz[a, z] = jnp.float32(fit_table[z, a])
 
     barrier = pltpu.get_barrier_semaphore()
     lo_block = (strip // group) * group
@@ -146,8 +169,6 @@
                 pl.when(down)(lambda: act(zcopy(0, h, i)))
 
     zsends(lambda c: c.start())
-    for copy in consts:
-        copy.start()
 
     def zwait(side, h):
         plane = jnp.where(side == 0, r - 1 - h, depth + r + h)
@@ -274,7 +295,7 @@
             for k, g in enumerate((gz, gy, gx)):
                 v = common * g
                 for a in range(knots_z):
-                    acc[a * 3 + k, tile, :] += v * fitz_ref[a, z]
+                    acc[a * 3 + k, tile, :] += v * fitz[a, z]
 
     from_sides(ycopy)
 
@@ -322,8 +343,9 @@
 
     for copy in consts:
         copy.wait()
-    reduced = dot(fity_ref[...], acc[...].reshape(knots_z * 3 * rows, width))
-    block = dot(reduced, fitx[...])
+    forces = halves(acc[...].reshape(knots_z * 3 * rows, width))
+    reduced = halves(dot3((fity[0], fity[1]), forces))
+    block = dot3(reduced, (fitx[0], fitx[1]))
     part[...] = block.reshape(part.shape)
 
     def pzcopy(side, dist):
@@ -400,8 +422,10 @@
             part[knots_y - count :] += part_y[1, dist - 1, 0:count]
 
     coef = part[...].reshape(flat) * weight
-    lines = dot(evalzy_ref[...], coef)
-    power = jnp.sum(lines * dot(lines, gram[...]))
+    lines = dot3(halves(coef), (evalx[0], evalx[1]))
+    high, low = halves(lines)
+    spread = jnp.concatenate([high, low, high], axis=0)
+    power = jnp.sum(lines * dot(gram[...], spread))
     power_out[0] = jnp.full((8, LANE), power, jnp.float32)
 
     size = n_z * group
@@ -416,9 +440,9 @@
 
     for step in range(1, size):
         wcopy(step, 0).start()
-    lines_per = lines.shape[0] // 3
+    voxels = depth * rows
     for k in range(3):
-        field_ref[k] = dot(lines[k * lines_per : (k + 1) * lines_per], evalx[...]).reshape(
+        field_ref[k] = dot(evalzy[k * voxels : (k + 1) * voxels, :], spread).reshape(
             depth, rows, width)
     total = power_out[0]
     for step in range(1, size):
@@ -450,25 +474,24 @@
     for step in range(1, groups):
         wcopy(step, 1).wait_send()
     entries = float(3 * depth * rows * width) * n_z * n_y
-    scale_ref[...] = 1.0 / (jnp.sqrt(total / entries) + 1e-06)
+    scale = 1.0 / (jnp.sqrt(total / entries) + 1e-06)
+    scale_ref[...] = jnp.broadcast_to(scale[0:1, 0:1], (rows, width))
 
 
 def shards(n_z, n_y, fixed, moving):
     depth, rows, width = fixed.shape
     r = RADIUS
-    eval_z, fit_z = np_tables(depth)
+    eval_z = np_tables(depth)[0]
     eval_y, fit_y = np_tables(rows)
     eval_x, fit_x = np_tables(width)
     knots_z, knots_y, knots_x = eval_z.shape[1], eval_y.shape[1], eval_x.shape[1]
     lines = knots_z * 3
     pad_rows = -(-lines // 8) * 8
     ctl_pad = -(-knots_x // LANE) * LANE
-    f32 = np.float32
     fitx = np.zeros((width, ctl_pad))
     fitx[:, :knots_x] = fit_x
     evalx = np.zeros((ctl_pad, width))
     evalx[:knots_x] = eval_x.T
-    gram = evalx @ evalx.T
     fity = np.zeros((knots_y, pad_rows, lines, rows))
     for line in range(lines):
         fity[:, line, line, :] = fit_y.T
@@ -478,22 +501,33 @@
         for a in range(knots_z):
             evalzy[k, :, :, :, a * 3 + k] = eval_z[:, a][:, None, None] * eval_y[None]
     evalzy = evalzy.reshape(3 * depth * rows, knots_y * pad_rows)
+    gram = evalzy.T @ evalzy
+
+    def thrice(table):
+        high, low = np_halves(table)
+        return jnp.asarray(np.concatenate([high, high, low], axis=1))
+
+    def both(table):
+        return jnp.asarray(np.stack(np_halves(table)))
+
     group = group_size(n_y)
     slots = n_z * group - 1 + n_y // group - 1
     reach_z = min((depth // SPACING + 2) // (depth // SPACING), n_z - 1)
     reach_y = min((rows // SPACING + 2) // (rows // SPACING), n_y - 1)
     dma = pltpu.SemaphoreType.DMA
     vmem = functools.partial(pltpu.VMEM, dtype=jnp.float32)
+    half = functools.partial(pltpu.VMEM, dtype=jnp.bfloat16)
+    lined = knots_y * pad_rows
     block = (knots_y, pad_rows, ctl_pad)
-    anywhere = pl.BlockSpec(memory_space=pl.ANY)
+    anywhere = pl.BlockSpec(memory_space=pltpu.HBM)
     inside = pl.BlockSpec(memory_space=pltpu.VMEM)
     field, scale = pl.pallas_call(
         functools.partial(kernel, n_z, n_y, depth, rows, width, group, ctl_pad),
         out_shape=(
             jax.ShapeDtypeStruct((3, depth, rows, width), jnp.float32),
-            jax.ShapeDtypeStruct((8, LANE), jnp.float32),
+            jax.ShapeDtypeStruct((rows, width), jnp.float32),
         ),
-        in_specs=[pl.BlockSpec(memory_space=pltpu.SMEM)] + [anywhere] * 5 + [inside] * 2,
+        in_specs=[anywhere] * 7,
         out_specs=(inside, inside),
         scratch_shapes=[
             vmem((2, depth + 2 * r, rows, width)),
@@ -502,15 +536,18 @@
             vmem((5, depth + 2 * r, rows, width)),
             vmem((depth + 2 * r, rows, width)),
             vmem((lines, rows, width)),
-            vmem((width, ctl_pad)),
-            vmem((ctl_pad, width)),
-            vmem((ctl_pad, ctl_pad)),
+            half((2, width, ctl_pad)),
+            half((2, ctl_pad, width)),
+            half((2, lined, lines * rows)),
+            half((3 * depth * rows, 3 * lined)),
+            half((lined, 3 * lined)),
+            pltpu.SMEM((knots_z, depth), jnp.float32),
             vmem(block),
             vmem((2, reach_z) + block),
             vmem((2, reach_y) + block),
             vmem((2, 8, LANE)),
             vmem((slots, 8, LANE)),
-            dma((2,)), dma((3,)),
+            dma((2,)), dma((5,)),
             dma((2, r, 2)), dma((2, r, 2)),
             dma((2,)), dma((2,)),
             dma((2, 2, r)), dma((2, 2, r)),
@@ -519,15 +556,13 @@
             dma((slots,)), dma((slots,)),
         ],
         compiler_params=pltpu.CompilerParams(
-            collective_id=0, has_side_effects=True, vmem_limit_bytes=48 * 1024 * 1024
+            collective_id=0, has_side_effects=True, vmem_limit_bytes=60 * 1024 * 1024
         ),
         cost_estimate=pl.CostEstimate(flops=10**9, bytes_accessed=10**7, transcendentals=0),
     )(
-        jnp.asarray(fit_z.T.astype(f32)), fixed, moving, jnp.asarray(fitx.astype(f32)),
-        jnp.asarray(evalx.astype(f32)), jnp.asarray(gram.astype(f32)),
-        jnp.asarray(fity.astype(f32)), jnp.asarray(evalzy.astype(f32)),
+        fixed, moving, both(fitx), both(evalx), both(fity), thrice(evalzy), thrice(gram),
     )
-    return field * scale[0, 0]
+    return field * scale[None, None]
 
 
 def solution(mesh):

time: 57.9 us -> 49.2 us (0.85)
  local copies, waits for them, and re-layouts: 8.55 us -> 0 us
  other arithmetic: 1.93 us -> 2.76 us
  Pallas kernels: 47 us -> 46.3 us
    unnamed x16 -> x0, local copies, waits for them, and re-layouts: 7.97 us -> none
    mul x1, other arithmetic: 1.93 us -> 2.76 us  [shards(): return field * scale[None, None]]
    pallas_call x1, Pallas kernels: 47 us -> 46.3 us  [shards(): pl.pallas_call(functools.partial(kernel, n_z, n_y, depth, rows, width, gr...]
    slice x1 -> x0, local copies, waits for them, and re-layouts: 0.58 us -> none  [shards(): return field * scale[0, 0]]
where the time goes in v2:
time: 49.2 us; the launch traced here: 49.1 us
  Pallas kernels  46.3 us (94%)
  other arithmetic  2.76 us (6%)
    pallas_call x1, Pallas kernels, shards(): pl.pallas_call(functools.partial(kernel, n_z, n_y, depth, rows, width, gr...  46.3 us
    mul x1, other arithmetic, shards(): return field * scale[None, None]  2.76 us

profile of v2, /device:TPU:0, one launch (start us, length us, event | category | flops | bytes accessed | tf_op | source)
XLA Modules:
  0.0 49.1 jit_solution(15305222345300893233)
XLA Ops:
  0.0 46.3 %shard_map.73 = (f32[3,8,16,1024]{3,2,1,0:T(8,128)}, f32[16,1024]{1,0:T(8,128)}) custom-call(f32[8,16,1024]{2,1,0:T(8,128)} %f_hbm.1, f32[8,16,1024]{2,1,0:T(8,128)} %m_hbm.1, bf16[2,1024,256]{2,1,0:T(8,128)(2,1)} %constant.10.clone.fitx_hbm, bf16[2,256,1024]{2,1,0:T(8,128)(2,1)} %constant.11.clone.evalx_hbm, bf16[2,80,192]{2,1,0:T(8,128)(2,1)} %constant.12.clone.fity_hbm, ...), custom_call_target="tpu_custom_call" | custom-call | flops 1000000000 | bytes 10000000 | tf_op jit(solution)/shard_map/pallas_call | solution.py:524
  46.3 2.8 %broadcast_multiply_fusion = f32[3,8,16,1024]{3,2,1,0:T(8,128)} fusion(f32[3,8,16,1024]{3,2,1,0:T(8,128)} %get-tuple-element.7, f32[16,1024]{1,0:T(8,128)} %get-tuple-element.8), kind=kLoop, calls=%fused_computation | loop fusion | flops 393216 | bytes 3211264 | tf_op jit(solution)/shard_map/mul | solution.py:565

commit v3 on v2

--- a/solution.py
+++ b/solution.py
@@ -326,16 +326,19 @@
         force_of(place(s))
         return carry
 
-    lax.fori_loop(0, depth - 2 * r, early, 0)
+    lax.fori_loop(0, depth - r, early, 0)
+
+    def pass_on(h, carry):
+        zwait(main, h)
+        pack(jnp.where(up, depth + r + h, r - 1 - h))
+        to_sides(lambda c: c.start(), lambda side: fcopy(side, main, h))
+        return carry
+
+    lax.fori_loop(0, r, pass_on, 0)
 
     def late(h, carry):
-        plane = jnp.where(up, depth + r + h, r - 1 - h)
-        zwait(main, h)
-        pack(plane)
-        to_sides(lambda c: c.start(), lambda side: fcopy(side, main, h))
-        force_of(place(depth - 2 * r + h))
         from_sides(lambda side: fcopy(side, main, h))
-        rows_of(plane)
+        rows_of(jnp.where(up, depth + r + h, r - 1 - h))
         force_of(place(depth - r + h))
         return carry
 

time: 49.2 us -> 44.9 us (0.913)
  Pallas kernels: 46.3 us -> 42 us
    pallas_call x1, Pallas kernels: 46.3 us -> 42 us  [shards(): pl.pallas_call(functools.partial(kernel, n_z, n_y, depth, rows, width, gr...]
where the time goes in v3:
time: 44.9 us; the launch traced here: 44.8 us
  Pallas kernels  42 us (94%)
  other arithmetic  2.76 us (6%)
    pallas_call x1, Pallas kernels, shards(): pl.pallas_call(functools.partial(kernel, n_z, n_y, depth, rows, width, gr...  42 us
    mul x1, other arithmetic, shards(): return field * scale[None, None]  2.76 us

profile of v3, /device:TPU:0, one launch (start us, length us, event | category | flops | bytes accessed | tf_op | source)
XLA Modules:
  0.0 44.8 jit_solution(18292471858702093788)
XLA Ops:
  0.0 42.0 %shard_map.73 = (f32[3,8,16,1024]{3,2,1,0:T(8,128)}, f32[16,1024]{1,0:T(8,128)}) custom-call(f32[8,16,1024]{2,1,0:T(8,128)} %f_hbm.1, f32[8,16,1024]{2,1,0:T(8,128)} %m_hbm.1, bf16[2,1024,256]{2,1,0:T(8,128)(2,1)} %constant.10.clone.fitx_hbm, bf16[2,256,1024]{2,1,0:T(8,128)(2,1)} %constant.11.clone.evalx_hbm, bf16[2,80,192]{2,1,0:T(8,128)(2,1)} %constant.12.clone.fity_hbm, ...), custom_call_target="tpu_custom_call" | custom-call | flops 1000000000 | bytes 10000000 | tf_op jit(solution)/shard_map/pallas_call | solution.py:527
  42.0 2.8 %broadcast_multiply_fusion = f32[3,8,16,1024]{3,2,1,0:T(8,128)} fusion(f32[3,8,16,1024]{3,2,1,0:T(8,128)} %get-tuple-element.7, f32[16,1024]{1,0:T(8,128)} %get-tuple-element.8), kind=kLoop, calls=%fused_computation | loop fusion | flops 393216 | bytes 3211264 | tf_op jit(solution)/shard_map/mul | solution.py:568

commit v4 on v3

--- a/solution.py
+++ b/solution.py
@@ -78,9 +78,9 @@
 
 def kernel(
     n_z, n_y, depth, rows, width, group, ctl_pad,
-    f_hbm, m_hbm, fitx_hbm, evalx_hbm, fity_hbm, evalzy_hbm, gram_hbm,
-    field_ref, scale_ref,
-    img, packout, packin, ysum, grady, acc, fitx, evalx, fity, evalzy, gram, fitz, part, part_z, part_y,
+    f_hbm, m_hbm, fitx_hbm, evalx_hbm, fity_hbm, gram_hbm,
+    spread_ref,
+    img, packout, packin, ysum, grady, acc, fitx, evalx, fity, gram, fitz, part, part_z, part_y,
     power_out, power_in,
     own_sem, const_sem, zs_sem, zr_sem, ys_sem, yr_sem, fs_sem, fr_sem,
     pzs_sem, pzr_sem, pys_sem, pyr_sem, ws_sem, wr_sem,
@@ -103,8 +103,7 @@
     consts = [
         pltpu.make_async_copy(src, dst, const_sem.at[i])
         for i, (src, dst) in enumerate(
-            ((fitx_hbm, fitx), (evalx_hbm, evalx), (fity_hbm, fity), (evalzy_hbm, evalzy),
-             (gram_hbm, gram))
+            ((fitx_hbm, fitx), (evalx_hbm, evalx), (fity_hbm, fity), (gram_hbm, gram))
         )
     ]
     for copy in own:
@@ -334,9 +333,13 @@
         to_sides(lambda c: c.start(), lambda side: fcopy(side, main, h))
         return carry
 
-    lax.fori_loop(0, r, pass_on, 0)
+    pass_on(0, 0)
 
     def late(h, carry):
+        @pl.when(h + 1 < r)
+        def _():
+            pass_on(h + 1, 0)
+
         from_sides(lambda side: fcopy(side, main, h))
         rows_of(jnp.where(up, depth + r + h, r - 1 - h))
         force_of(place(depth - r + h))
@@ -443,10 +446,6 @@
 
     for step in range(1, size):
         wcopy(step, 0).start()
-    voxels = depth * rows
-    for k in range(3):
-        field_ref[k] = dot(evalzy[k * voxels : (k + 1) * voxels, :], spread).reshape(
-            depth, rows, width)
     total = power_out[0]
     for step in range(1, size):
         wcopy(step, 0).wait_recv()
@@ -478,7 +477,12 @@
         wcopy(step, 1).wait_send()
     entries = float(3 * depth * rows * width) * n_z * n_y
     scale = 1.0 / (jnp.sqrt(total / entries) + 1e-06)
-    scale_ref[...] = jnp.broadcast_to(scale[0:1, 0:1], (rows, width))
+    high, low = halves(lines * scale[0:1, 0:1])
+    spread_ref[...] = jnp.concatenate([high, low, high], axis=0)
+
+
+def field_kernel(table_ref, spread_ref, out_ref):
+    out_ref[...] = dot(table_ref[...], spread_ref[...]).reshape(out_ref.shape)
 
 
 def shards(n_z, n_y, fixed, moving):
@@ -524,14 +528,11 @@
     block = (knots_y, pad_rows, ctl_pad)
     anywhere = pl.BlockSpec(memory_space=pltpu.HBM)
     inside = pl.BlockSpec(memory_space=pltpu.VMEM)
-    field, scale = pl.pallas_call(
+    spread = pl.pallas_call(
         functools.partial(kernel, n_z, n_y, depth, rows, width, group, ctl_pad),
-        out_shape=(
-            jax.ShapeDtypeStruct((3, depth, rows, width), jnp.float32),
-            jax.ShapeDtypeStruct((rows, width), jnp.float32),
-        ),
-        in_specs=[anywhere] * 7,
-        out_specs=(inside, inside),
+        out_shape=jax.ShapeDtypeStruct((3 * lined, width), jnp.bfloat16),
+        in_specs=[anywhere] * 6,
+        out_specs=inside,
         scratch_shapes=[
             vmem((2, depth + 2 * r, rows, width)),
             vmem((2, depth + 2 * r, 8, width)),
@@ -542,7 +543,6 @@
             half((2, width, ctl_pad)),
             half((2, ctl_pad, width)),
             half((2, lined, lines * rows)),
-            half((3 * depth * rows, 3 * lined)),
             half((lined, 3 * lined)),
             pltpu.SMEM((knots_z, depth), jnp.float32),
             vmem(block),
@@ -550,7 +550,7 @@
             vmem((2, reach_y) + block),
             vmem((2, 8, LANE)),
             vmem((slots, 8, LANE)),
-            dma((2,)), dma((5,)),
+            dma((2,)), dma((4,)),
             dma((2, r, 2)), dma((2, r, 2)),
             dma((2,)), dma((2,)),
             dma((2, 2, r)), dma((2, 2, r)),
@@ -563,9 +563,19 @@
         ),
         cost_estimate=pl.CostEstimate(flops=10**9, bytes_accessed=10**7, transcendentals=0),
     )(
-        fixed, moving, both(fitx), both(evalx), both(fity), thrice(evalzy), thrice(gram),
+        fixed, moving, both(fitx), both(evalx), both(fity), thrice(gram),
     )
-    return field * scale[None, None]
+    return pl.pallas_call(
+        field_kernel,
+        out_shape=jax.ShapeDtypeStruct((3, depth, rows, width), jnp.float32),
+        grid=(3,),
+        in_specs=[
+            pl.BlockSpec((depth * rows, 3 * lined), lambda k: (k, 0)),
+            pl.BlockSpec((3 * lined, width), lambda k: (0, 0)),
+        ],
+        out_specs=pl.BlockSpec((1, depth, rows, width), lambda k: (k, 0, 0, 0)),
+        compiler_params=pltpu.CompilerParams(vmem_limit_bytes=32 * 1024 * 1024),
+    )(thrice(evalzy), spread)
 
 
 def solution(mesh):

time: 44.9 us -> 46.3 us (1.031)
  Pallas kernels: 42 us -> 45.1 us
  other arithmetic: 2.76 us -> 0 us
  local copies, waits for them, and re-layouts: 0 us -> 1.03 us
    mul x1 -> x0, other arithmetic: 2.76 us -> none  [shards(): return field * scale[None, None]]
    pallas_call x0 -> x1, Pallas kernels: none -> 2.04 us  [shards(): pl.pallas_call(field_kernel, out_shape=jax.ShapeDtypeStruct((3, depth, ro...]
    pallas_call x1, Pallas kernels: 42 us -> 43.1 us  [shards(): pl.pallas_call(functools.partial(kernel, n_z, n_y, depth, rows, width, gr...]
    unnamed x0 -> x4, local copies, waits for them, and re-layouts: none -> 1.03 us
where the time goes in v4:
time: 46.3 us; the launch traced here: 46.2 us
  Pallas kernels  45.1 us (97%)
  local copies, waits for them, and re-layouts  1.03 us (2%)
    pallas_call x1, Pallas kernels, shards(): pl.pallas_call(functools.partial(kernel, n_z, n_y, depth, rows, width, gr...  43.1 us
    pallas_call x1, Pallas kernels, shards(): pl.pallas_call(field_kernel, out_shape=jax.ShapeDtypeStruct((3, depth, ro...  2.04 us
    unnamed x4, local copies, waits for them, and re-layouts  1.03 us

profile of v4, /device:TPU:0, one launch (start us, length us, event | category | flops | bytes accessed | tf_op | source)
XLA Modules:
  0.0 46.2 jit_solution(16896270990449841354)
XLA Ops:
  0.0 0.0 copy-start.1
  0.0 43.1 %shard_map.73.spread_ref = bf16[240,1024]{1,0:T(8,128)(2,1)} custom-call(f32[8,16,1024]{2,1,0:T(8,128)} %f_hbm.1, f32[8,16,1024]{2,1,0:T(8,128)} %m_hbm.1, bf16[2,1024,256]{2,1,0:T(8,128)(2,1)} %constant.10.clone.fitx_hbm, bf16[2,256,1024]{2,1,0:T(8,128)(2,1)} %constant.11.clone.evalx_hbm, bf16[2,80,192]{2,1,0:T(8,128)(2,1)} %constant.12.clone.fity_hbm, ...), custom_call_target="tpu_custom_call" | custom-call | flops 1000000000 | bytes 10000000 | tf_op jit(solution)/shard_map/pallas_call | solution.py:531
  43.1 0.0 copy-done.1
  43.1 0.0 copy-start
  43.1 1.0 %copy-done = bf16[240,1024]{1,0:T(8,128)(2,1)S(1)} copy-done((bf16[240,1024]{1,0:T(8,128)(2,1)S(1)}, bf16[240,1024]{1,0:T(8,128)(2,1)}, u32[]{:S(2)}) %copy-start) | copy-done | bytes 491544
  44.1 2.0 %shard_map.74 = f32[3,8,16,1024]{3,2,1,0:T(8,128)} custom-call(bf16[384,240]{1,0:T(8,128)(2,1)S(1)} %copy-done.1, bf16[240,1024]{1,0:T(8,128)(2,1)S(1)} %copy-done), custom_call_target="tpu_custom_call" | custom-call | tf_op jit(solution)/shard_map/pallas_call | solution.py:568
Async XLA Ops:
  0.0 43.1 %copy-start.1 = (bf16[384,240]{1,0:T(8,128)(2,1)S(1)}, bf16[384,240]{1,0:T(8,128)(2,1)}, u32[]{:S(2)}) copy-start(bf16[384,240]{1,0:T(8,128)(2,1)} %constant.14.clone.table_ref) | copy-start | bytes 552964
  43.1 1.0 %copy-start = (bf16[240,1024]{1,0:T(8,128)(2,1)S(1)}, bf16[240,1024]{1,0:T(8,128)(2,1)}, u32[]{:S(2)}) copy-start(bf16[240,1024]{1,0:T(8,128)(2,1)} %shard_map.73.spread_ref) | copy-start | bytes 1474564

commit v5 on v3

--- a/solution.py
+++ b/solution.py
@@ -326,7 +326,7 @@
         force_of(place(s))
         return carry
 
-    lax.fori_loop(0, depth - r, early, 0)
+    lax.fori_loop(0, (depth - r) // 2, early, 0)
 
     def pass_on(h, carry):
         zwait(main, h)
@@ -335,6 +335,7 @@
         return carry
 
     lax.fori_loop(0, r, pass_on, 0)
+    lax.fori_loop((depth - r) // 2, depth - r, early, 0)
 
     def late(h, carry):
         from_sides(lambda side: fcopy(side, main, h))

time: 44.9 us -> 45.2 us (level)
  no operation moved by 1% of the time
where the time goes in v5:
time: 45.2 us; the launch traced here: 45.1 us
  Pallas kernels  42.3 us (94%)
  other arithmetic  2.76 us (6%)
    pallas_call x1, Pallas kernels, shards(): pl.pallas_call(functools.partial(kernel, n_z, n_y, depth, rows, width, gr...  42.3 us
    mul x1, other arithmetic, shards(): return field * scale[None, None]  2.76 us

profile of v5, /device:TPU:0, one launch (start us, length us, event | category | flops | bytes accessed | tf_op | source)
XLA Modules:
  0.0 45.1 jit_solution(4012414170855544264)
XLA Ops:
  0.0 42.3 %shard_map.73 = (f32[3,8,16,1024]{3,2,1,0:T(8,128)}, f32[16,1024]{1,0:T(8,128)}) custom-call(f32[8,16,1024]{2,1,0:T(8,128)} %f_hbm.1, f32[8,16,1024]{2,1,0:T(8,128)} %m_hbm.1, bf16[2,1024,256]{2,1,0:T(8,128)(2,1)} %constant.10.clone.fitx_hbm, bf16[2,256,1024]{2,1,0:T(8,128)(2,1)} %constant.11.clone.evalx_hbm, bf16[2,80,192]{2,1,0:T(8,128)(2,1)} %constant.12.clone.fity_hbm, ...), custom_call_target="tpu_custom_call" | custom-call | flops 1000000000 | bytes 10000000 | tf_op jit(solution)/shard_map/pallas_call | solution.py:528
  42.3 2.8 %broadcast_multiply_fusion = f32[3,8,16,1024]{3,2,1,0:T(8,128)} fusion(f32[3,8,16,1024]{3,2,1,0:T(8,128)} %get-tuple-element.7, f32[16,1024]{1,0:T(8,128)} %get-tuple-element.8), kind=kLoop, calls=%fused_computation | loop fusion | flops 393216 | bytes 3211264 | tf_op jit(solution)/shard_map/mul | solution.py:569
